TPU v7x, 512 devices: a whole 4x8x8 slice. The times are simulated.
512 devices in a mesh: tile: 32 (over y, z_lo, core), trc: 16 (over x, z_hi).
Axes of the slice: x: 4, y: 8, z: 8 (z_hi: 4, z_lo: 2; z = z_hi * 2 + z_lo), core: 2. Of those that a mesh axis runs over, the one named last changes fastest.
Arguments:
- tracers: float32 [512, 128, 2, 128], P('trc', 'tile'), may hold values from 0.05 to 2
- courant: float32 [3, 128, 2, 128], P(None, 'tile', None, 'trc'), may hold values from -6 to 6
- shear: float32 [3, 128, 2, 128], P(None, 'tile', None, 'trc'), may hold values from -8 to 8
- offsets: int32 [3, 128, 2, 128], P(None, 'tile'), may hold values from -1 to 0
- seam_flips: int32 [32], replicated, may hold values from 0 to 1
- kernel: float32 [32, 32], replicated, may hold values from 0.0005 to 0.004
- coag_target: int32 [32, 32], replicated, may hold values from 0 to 31, as said below
Outputs:
- updated: float32 [512, 128, 2, 128], P('trc', 'tile')
Inputs may be any that keep to these rules, and one draw needn't show every extreme that they name: coag_target[i, j] lies between max(i, j) and 31.
All inputs are finite; a program needn't handle non-finite values.
Results may differ from a plain program's by a relative error of at most 0.00014.
Values sent between devices are 32-bit elements; how exact they have to be, the bound alone decides.
A program may use at most 64 MiB of HBM per device.

v0:
```python
import jax
import jax.numpy as jnp
from jax import lax
from jax.sharding import Mesh
from jax.sharding import PartitionSpec as P

BINS = 32
COMPS = 16
ITER = 3
TRC = ("trc_0", "trc_1")


precise = lax.Precision.HIGHEST


def gather_turned(arrays, axis, dims):
    turned = [jnp.moveaxis(a, dim, 0) for a, dim in zip(arrays, dims)]
    both = jnp.concatenate([t.reshape(len(t), -1) for t in turned], axis=1)
    result, at, gathered = (lax.all_gather(both, axis, axis=0, tiled=True), 0, [])
    for t, dim in zip(turned, dims):
        piece = result[:, at : at + t[0].size].reshape(-1, *t.shape[1:])
        gathered.append(jnp.moveaxis(piece, 0, dim))
        at += t[0].size
    return tuple(gathered)


def with_halo(cells, sides, width):
    for axis, dim in sides:
        count = lax.axis_size(axis)
        head = lax.slice_in_dim(cells, 0, width, axis=dim)
        tail = lax.slice_in_dim(cells, cells.shape[dim] - width, cells.shape[dim], axis=dim)
        cells = jnp.concatenate(
            [
                lax.ppermute(tail, axis, [(i, (i + 1) % count) for i in range(count)]),
                cells,
                lax.ppermute(head, axis, [((i + 1) % count, i) for i in range(count)]),
            ],
            axis=dim,
        )
    return cells


def split_up(array, dim, length):
    before, after = (array.shape[:dim], array.shape[dim + 1 :])
    return jnp.moveaxis(array.reshape(*before, length, -1, *after), dim, 0)


def joined_along(tiles, dim):
    tiles = jnp.moveaxis(tiles, 0, dim)
    shape = tiles.shape
    return tiles.reshape(*shape[:dim], shape[dim] * shape[dim + 1], *shape[dim + 2 :])


def moved_by_axis(tiles, axes, sequence):
    inside = tiles.shape[1:]
    result = tiles.reshape(*(lax.axis_size(a) for a in axes), *inside)
    for k in sequence:
        result = lax.all_to_all(result, axes[k], k, k, tiled=True)
    return result.reshape(-1, *inside)


def stepwise_exchange(array, axes, sequence, split_dim, concat_dim):
    tiles = split_up(array, split_dim, lax.axis_size(axes))
    return joined_along(moved_by_axis(tiles, axes, sequence), concat_dim)


def fractions(courant, shear):
    fraction = jnp.full(courant.shape, 0.5, jnp.float32)
    for repeat in range(ITER):
        fraction = jax.nn.sigmoid(courant + shear * (fraction - 0.5))
    return fraction


def cubic_taps(fraction, offsets):
    first_node = -fraction * (fraction - 1.0) * (fraction - 2.0) / 6.0
    second_node = (fraction + 1.0) * (fraction - 1.0) * (fraction - 2.0) / 2.0
    third_node = -(fraction + 1.0) * fraction * (fraction - 2.0) / 2.0
    fourth_node = (fraction + 1.0) * fraction * (fraction - 1.0) / 6.0
    zeros = jnp.zeros_like(fraction)
    lower = offsets == -1
    weights = [
        jnp.where(lower, first_node, zeros),
        jnp.where(lower, second_node, first_node),
        jnp.where(lower, third_node, second_node),
        jnp.where(lower, fourth_node, third_node),
        jnp.where(lower, zeros, fourth_node),
    ]
    return jnp.stack(weights, axis=1)


def interpolate(padded, stencil):
    cross, levels, along = (stencil.shape[2], stencil.shape[3], stencil.shape[4])
    summed = jnp.zeros((padded.shape[0], cross, levels, along), jnp.float32)
    for x_step in range(5):
        for l_step in range(5):
            partial_sum = jnp.zeros((padded.shape[0], cross, levels, along), jnp.float32)
            for y_step in range(5):
                partial_sum = (
                    partial_sum
                    + stencil[2, y_step]
                    * padded[
                        :,
                        x_step : x_step + cross,
                        l_step : l_step + levels,
                        y_step : y_step + along,
                    ]
                )
            summed = summed + stencil[0, x_step] * stencil[1, l_step] * partial_sum
    return summed


def coagulate(masses, kernel, coag_target):
    number = jnp.sum(jnp.abs(masses), axis=1)
    losses = jnp.dot(kernel, number, precision=precise, preferred_element_type=jnp.float32)
    bin_index = jnp.arange(BINS, dtype=jnp.int32)
    matches = (coag_target[None, :, :] == bin_index[:, None, None]).astype(jnp.float32)
    redistribute = (matches * kernel[None, :, :]).reshape(BINS * BINS, BINS)
    transfer_rate = jnp.dot(
        redistribute, number, precision=precise, preferred_element_type=jnp.float32
    )
    transfer_rate = transfer_rate.reshape(BINS, BINS, number.shape[1])
    gained = jnp.einsum("bic,ikc->bkc", transfer_rate, masses, precision=precise)
    return (masses + gained) / (1.0 + losses[:, None, :])


def on_device(tracers, courant, shear, offsets, seam_flips, kernel, coag_target):
    gathered_courant, gathered_shear = gather_turned((courant, shear), TRC, (3, 3))
    stencil = cubic_taps(fractions(gathered_courant, gathered_shear), offsets)
    tile_index = lax.axis_index("tile")
    tile_count = lax.axis_size("tile")
    left_flag = lax.dynamic_index_in_dim(seam_flips, tile_index, 0, False) == 1
    right_flag = lax.dynamic_index_in_dim(seam_flips, (tile_index + 1) % tile_count, 0, False) == 1

    def widen(tracer_field):
        padded = with_halo(tracer_field, (("tile", 1),), 2)
        left_rim = padded[:, :2]
        right_rim = padded[:, -2:]
        left_rim = jnp.where(left_flag, left_rim[..., ::-1], left_rim)
        right_rim = jnp.where(right_flag, right_rim[..., ::-1], right_rim)
        widened = jnp.concatenate([left_rim, tracer_field, right_rim], axis=1)
        widened = jnp.pad(widened, ((0, 0), (0, 0), (2, 2), (0, 0)), mode="edge")
        return jnp.pad(widened, ((0, 0), (0, 0), (0, 0), (2, 2)), mode="wrap")

    moved_once = interpolate(widen(tracers), stencil)
    padded = widen(moved_once)
    moved_twice = interpolate(padded, stencil)
    cell_field = lax.all_to_all(moved_twice, TRC, split_axis=3, concat_axis=0, tiled=True)
    masses = cell_field.reshape(BINS, COMPS, -1)
    coagulated = coagulate(masses, kernel, coag_target).reshape(cell_field.shape)
    return stepwise_exchange(coagulated, TRC, (0, 1), 0, 3)


def solution(mesh):
    torus = Mesh(mesh.devices.reshape(mesh.shape["tile"], 4, 4), ("tile", "trc_0", "trc_1"))
    return jax.shard_map(
        on_device,
        mesh=torus,
        in_specs=(
            P(TRC, "tile", None, None),
            P(None, "tile", None, TRC),
            P(None, "tile", None, TRC),
            P(None, "tile", None, None),
            P(),
            P(),
            P(),
        ),
        out_specs=P(TRC, "tile", None, None),
        check_vma=False,
    )
```

profile of v0, /device:TPU:6, one launch (start us, length us, event | category | flops | bytes accessed | tf_op | source)
XLA Modules:
  0.0 143.8 jit_solution(2569679894787739675)
XLA Ops:
  0.0 1.0 copy.1192
  1.0 1.9 %collective-permute-start = (f32[32,2,2,128]{3,0,2,1:T(8,128)S(1)}, f32[32,2,2,128]{3,0,2,1:T(8,128)S(1)}, u32[]{:S(2)}, u32[]{:S(2)}) collective-permute-start(f32[32,2,2,128]{3,0,2,1:T(8,128)S(1)} %get-tuple-element.266), channel_id=1, source_target_pairs={{0,16},{16,32},{32,48},{48,64},{64,80},{80,96},{96,112},{112,128},... | collective-permute-start | bytes 196616 | tf_op jit(solution)/shard_map/ppermute | solution.py:34
  3.0 6.6 %collective-permute-start.1 = (f32[32,2,2,128]{3,0,2,1:T(8,128)S(1)}, f32[32,2,2,128]{3,0,2,1:T(8,128)S(1)}, u32[]{:S(2)}, u32[]{:S(2)}) collective-permute-start(f32[32,2,2,128]{3,0,2,1:T(8,128)S(1)} %get-tuple-element.267), channel_id=1, source_target_pairs={{16,0},{32,16},{48,32},{64,48},{80,64},{96,80},{112,96},{128,112},... | collective-permute-start | bytes 196616 | tf_op jit(solution)/shard_map/ppermute | solution.py:36
  11.2 41.9 %all_gather.3 = f32[128,48]{1,0:T(8,128)S(1)} all-gather(f32[8,48]{1,0:T(8,128)S(1)} %pad_maximum_fusion.12), channel_id=1, replica_groups=mesh['tile'=32,'trc_0'=4,'trc_1'=4] {'trc_0','trc_1'}, dimensions={0}, use_global_device_ids=true | all-gather | bytes 26112 | tf_op jit(solution)/shard_map/all_gather | solution.py:19
  53.3 0.8 broadcast_select_fusion.5
  57.5 0.9 maximum_maximum_fusion
  58.4 0.9 fusion.335
  59.2 0.9 fusion.336
  60.2 1.4 fusion.337
  61.5 1.3 fusion.338
  63.4 0.9 fusion.340
  64.8 4.7 %fusion.55 = f32[32,4,2,128]{3,0,2,1:T(8,128)S(1)} fusion(f32[32,4,2,128]{3,0,2,1:T(8,128)S(1)} %copy.1192, f32[32,2,2,128]{3,0,2,1:T(8,128)S(1)} %broadcast_select_fusion.1, f32[32,2,2,128]{3,0,2,1:T(8,128)S(1)} %broadcast_select_fusion.3, f32[32,4,2,128]{3,1,2,0:T(4,128)S(1)} %get-tuple-element.207, f32[32,4,2,128]{3,1,2,0:T(4,128)S(1)} %get-tuple-element.147, ...), kind=kLoop, calls=%fused_computation.80 | loop fusion | flops 9109504 | bytes 15589376 | tf_op jit(solution)/shard_map/add | solution.py:108
  69.5 1.9 %collective-permute-start.2 = (f32[32,2,2,128]{3,0,2,1:T(8,128)S(1)}, f32[32,2,2,128]{3,0,2,1:T(8,128)S(1)}, u32[]{:S(2)}, u32[]{:S(2)}) collective-permute-start(f32[32,2,2,128]{3,0,2,1:T(8,128)S(1)} %get-tuple-element.254), channel_id=1, source_target_pairs={{0,16},{16,32},{32,48},{48,64},{64,80},{80,96},{96,112},{112,128},... | collective-permute-start | bytes 196616 | tf_op jit(solution)/shard_map/ppermute | solution.py:34
  71.5 5.9 %collective-permute-start.3 = (f32[32,2,2,128]{3,0,2,1:T(8,128)S(1)}, f32[32,2,2,128]{3,0,2,1:T(8,128)S(1)}, u32[]{:S(2)}, u32[]{:S(2)}) collective-permute-start(f32[32,2,2,128]{3,0,2,1:T(8,128)S(1)} %get-tuple-element.255), channel_id=1, source_target_pairs={{16,0},{32,16},{48,32},{64,48},{80,64},{96,80},{112,96},{128,112},... | collective-permute-start | bytes 196616 | tf_op jit(solution)/shard_map/ppermute | solution.py:36
  77.6 1.5 %collective-permute-done.3 = f32[32,2,2,128]{3,0,2,1:T(8,128)S(1)} collective-permute-done((f32[32,2,2,128]{3,0,2,1:T(8,128)S(1)}, f32[32,2,2,128]{3,0,2,1:T(8,128)S(1)}, u32[]{:S(2)}, u32[]{:S(2)}) %collective-permute-start.3) | collective-permute-done | bytes 65568 | tf_op jit(solution)/shard_map/ppermute | solution.py:36
  80.1 0.9 maximum_maximum_fusion.1
  81.0 0.9 fusion.329
  81.9 0.9 fusion.330
  82.8 1.4 fusion.331
  84.2 1.3 fusion.332
  85.5 0.9 fusion.334
  87.4 4.7 %fusion.20 = f32[32,4,2,128]{3,0,2,1:T(8,128)S(1)} fusion(f32[32,4,2,128]{3,0,2,1:T(8,128)S(1)} %fusion.55, f32[32,2,2,128]{3,0,2,1:T(8,128)S(1)} %broadcast_select_fusion, f32[32,2,2,128]{3,0,2,1:T(8,128)S(1)} %broadcast_select_fusion.2, f32[32,4,2,128]{3,1,2,0:T(4,128)S(1)} %get-tuple-element.107, f32[32,4,2,128]{3,1,2,0:T(4,128)S(1)} %get-tuple-element.47, ...), kind=kLoop, calls=%fused_computation.45 | loop fusion | flops 9109504 | bytes 15589376 | tf_op jit(solution)/shard_map/add | solution.py:108
  93.1 18.1 %all_to_all.25 = f32[16,1,2048]{2,1,0:T(1,128)S(1)} all-to-all(f32[16,1,2048]{2,1,0:T(1,128)S(1)} %reshape.181), channel_id=1, replica_groups=mesh['tile'=32,'trc_0'=4,'trc_1'=4] {'trc_0','trc_1'}, dimensions={0} | all-to-all | bytes 262144 | tf_op jit(solution)/shard_map/all_to_all | solution.py:147
  111.7 0.9 reduce
  115.2 0.9 copy.1448
  116.2 1.8 %fusion.355 = f32[64,16,32]{2,1,0:T(8,128)S(1)} fusion(f32[32,16,64]{1,0,2:T(8,128)S(1)} %reshape.157, f32[32,32,64]{1,0,2:T(8,128)S(1)} %copy.1448), kind=kOutput, calls=%fused_computation.653 | convolution fusion | flops 12582912 | bytes 524288 | tf_op jit(solution)/shard_map/bic,ikc->bkc/dot_general | solution.py:122
  118.3 0.9 copy.1451
  120.1 8.7 %all_to_all.26 = f32[4,1,8192]{2,1,0:T(1,128)S(1)} all-to-all(f32[4,1,8192]{2,1,0:T(1,128)S(1)} %reshape.183), channel_id=1, replica_groups=mesh['tile'=32,'trc_0'=4,'trc_1'=4] {'trc_0'}, dimensions={0} | all-to-all | bytes 262144 | tf_op jit(solution)/shard_map/all_to_all | solution.py:58
  128.8 1.0 reduce.1
  130.7 10.8 %all_to_all.27 = f32[4,1,8192]{2,1,0:T(1,128)S(1)} all-to-all(f32[4,1,8192]{2,1,0:T(1,128)S(1)} %reshape.185), channel_id=1, replica_groups=mesh['tile'=32,'trc_0'=4,'trc_1'=4] {'trc_1'}, dimensions={0} | all-to-all | bytes 262144 | tf_op jit(solution)/shard_map/all_to_all | solution.py:58
  141.6 1.0 reduce.2
  142.9 0.8 copy.1456
  (101 shorter events, 13.0 us)
Async XLA Ops:
  0.0 54.3 %copy-start = (f32[32,4,2,128]{3,2,1,0:T(2,128)S(1)}, f32[32,4,2,128]{3,2,1,0:T(2,128)}, u32[]{:S(2)}) copy-start(f32[32,4,2,128]{3,2,1,0:T(2,128)} %param.7) | copy-start | bytes 393220
  0.0 54.3 %copy-start.3 = (s32[32]{0:T(128)S(1)}, s32[32]{0:T(128)}, u32[]{:S(2)}) copy-start(s32[32]{0:T(128)} %param.11) | copy-start | bytes 388
  1.0 55.3 %collective-permute-start = (f32[32,2,2,128]{3,0,2,1:T(8,128)S(1)}, f32[32,2,2,128]{3,0,2,1:T(8,128)S(1)}, u32[]{:S(2)}, u32[]{:S(2)}) collective-permute-start(f32[32,2,2,128]{3,0,2,1:T(8,128)S(1)} %get-tuple-element.266), channel_id=1, source_target_pairs={{0,16},{16,32},{32,48},{48,64},{64,80},{80,96},{96,112},{112,128},... | collective-permute-start | bytes 196616 | tf_op jit(solution)/shard_map/ppermute | solution.py:34
  3.0 53.6 %collective-permute-start.1 = (f32[32,2,2,128]{3,0,2,1:T(8,128)S(1)}, f32[32,2,2,128]{3,0,2,1:T(8,128)S(1)}, u32[]{:S(2)}, u32[]{:S(2)}) collective-permute-start(f32[32,2,2,128]{3,0,2,1:T(8,128)S(1)} %get-tuple-element.267), channel_id=1, source_target_pairs={{16,0},{32,16},{48,32},{64,48},{80,64},{96,80},{112,96},{128,112},... | collective-permute-start | bytes 196616 | tf_op jit(solution)/shard_map/ppermute | solution.py:36
  69.5 8.0 %collective-permute-start.2 = (f32[32,2,2,128]{3,0,2,1:T(8,128)S(1)}, f32[32,2,2,128]{3,0,2,1:T(8,128)S(1)}, u32[]{:S(2)}, u32[]{:S(2)}) collective-permute-start(f32[32,2,2,128]{3,0,2,1:T(8,128)S(1)} %get-tuple-element.254), channel_id=1, source_target_pairs={{0,16},{16,32},{32,48},{48,64},{64,80},{80,96},{96,112},{112,128},... | collective-permute-start | bytes 196616 | tf_op jit(solution)/shard_map/ppermute | solution.py:34
  71.5 7.6 %collective-permute-start.3 = (f32[32,2,2,128]{3,0,2,1:T(8,128)S(1)}, f32[32,2,2,128]{3,0,2,1:T(8,128)S(1)}, u32[]{:S(2)}, u32[]{:S(2)}) collective-permute-start(f32[32,2,2,128]{3,0,2,1:T(8,128)S(1)} %get-tuple-element.255), channel_id=1, source_target_pairs={{16,0},{32,16},{48,32},{64,48},{80,64},{96,80},{112,96},{128,112},... | collective-permute-start | bytes 196616 | tf_op jit(solution)/shard_map/ppermute | solution.py:36
  113.5 1.0 copy-start.1
  113.5 1.1 copy-start.2
where the time goes:
time: 146 us; the launch traced here: 144 us
  blocking collectives  79.6 us (55%)
  local copies, waits for them, and re-layouts  25.3 us (17%)
  starting transfers between devices  16.4 us (11%)
  other arithmetic  16.4 us (11%)
  matrix products  2.54 us (2%)
  between operations  2.12 us (1%)
  waiting for transfers between devices  1.54 us (1%)
    all_gather x1, blocking collectives, gather_turned(): lax.all_gather(both, axis, axis=0, tiled=True)  41.9 us
    all_to_all x2, blocking collectives, moved_by_axis(): result = lax.all_to_all(result, axes[k], k, k, tiled=True)  19.5 us
    all_to_all x1, blocking collectives, on_device(): lax.all_to_all(moved_twice, TRC, split_axis=3, concat_axis=0, tiled=True)  18.1 us
    slice x38, local copies, waits for them, and re-layouts, interpolate(): padded[:, x_step:x_step + cross, l_step:l_step + levels, y_step:y_step +...  12.6 us
    ppermute x2, starting transfers between devices, with_halo(): lax.ppermute(head, axis, [((i + 1) % count, i) for i in range(count)])  12.6 us
    add x2, other arithmetic, interpolate(): summed = summed + stencil[0, x_step] * stencil[1, l_step] * partial_sum  9.42 us
    ppermute x2, starting transfers between devices, with_halo(): lax.ppermute(tail, axis, [(i, (i + 1) % count) for i in range(count)])  3.84 us
    unnamed x18, local copies, waits for them, and re-layouts  3.43 us
  transfers between devices with their start and end apart: 4, of which 1 were waited for; matrix products, arithmetic and copies ran while one was open for 3% of the time, Pallas kernels for 0%

commit v1 on v0

v1 whole, which is shorter than its diff:
```python
import functools

import jax
import jax.numpy as jnp
from jax import lax
from jax.experimental import pallas as pl
from jax.experimental.pallas import tpu as pltpu
from jax.sharding import PartitionSpec as P

BINS = 32
COMPS = 16
ITER = 3
TRC = 16
SIDE = 4
MESH = pl.DeviceIdType.MESH
EXACT = lax.Precision.HIGHEST


def taps(f, lower):
    p0 = -f * (f - 1.0) * (f - 2.0) / 6.0
    p1 = (f + 1.0) * (f - 1.0) * (f - 2.0) / 2.0
    p2 = -(f + 1.0) * f * (f - 2.0) / 2.0
    p3 = (f + 1.0) * f * (f - 1.0) / 6.0
    zero = jnp.zeros_like(f)
    return [
        jnp.where(lower, p0, zero),
        jnp.where(lower, p1, p0),
        jnp.where(lower, p2, p1),
        jnp.where(lower, p3, p2),
        jnp.where(lower, zero, p3),
    ]


def transport(src, wbuf, x):
    out = None
    for b in range(5):
        acc = [[None] * 4, [None] * 4]
        for a in range(5):
            for level in range(2):
                q = [src[2 * x + 2 * a + level, pl.ds(8 * g, 8), :] for g in range(4)]
                for l in range(2):
                    w = wbuf[(b * 5 + a) * 2 + level, pl.ds(2 * x + l, 1), :]
                    w = jnp.broadcast_to(w, (8, 128))
                    for g in range(4):
                        term = w * q[g]
                        acc[l][g] = term if acc[l][g] is None else acc[l][g] + term
        if b != 2:
            acc = [[pltpu.roll(v, (2 - b) % 128, 1) for v in row] for row in acc]
        out = acc if out is None else [[o + v for o, v in zip(r, s)] for r, s in zip(out, acc)]
    return out


def body(
    n_tile, tr, co, sh, of, fl, ke, ct, out,
    tin, cin, sin, oin, kin, ctin, fpad, fsend, frecv, wbuf, src1, src2,
    send2, recv2, abuf, nbuf, tbuf, rbuf, send3, recv3,
    in_sem, hs_sem, hr_sem, fs_sem, fr_sem, s2_sem, r2_sem, s3_sem, r3_sem,
):
    tile, me = lax.axis_index("tile"), lax.axis_index("trc")
    x_me, z_me = me // SIDE, lax.rem(me, SIDE)
    prev = lax.rem(tile + n_tile - 1, n_tile)
    after = lax.rem(tile + 1, n_tile)

    loads = [
        pltpu.make_async_copy(s, d, in_sem.at[i])
        for i, (s, d) in enumerate(
            ((co, cin), (sh, sin), (tr, tin), (of, oin), (ke, kin), (ct, ctin))
        )
    ]
    for load in loads:
        load.start()

    barrier = pltpu.get_barrier_semaphore()
    for k in range(1, TRC):
        pl.semaphore_signal(barrier, inc=1, device_id=(tile, lax.rem(me + k, TRC)), device_id_type=MESH)
    for t in (prev, after):
        pl.semaphore_signal(barrier, inc=1, device_id=(t, me), device_id_type=MESH)

    lane = lax.broadcasted_iota(jnp.int32, (8, 128), 1)
    sub = lax.broadcasted_iota(jnp.int32, (8, 128), 0)
    low = lane < 64

    fpad[...] = jnp.zeros_like(fpad)
    loads[0].wait()
    loads[1].wait()
    c, s = cin[...], sin[...]
    f = jnp.full(c.shape, 0.5, jnp.float32)
    for _ in range(ITER):
        f = jax.nn.sigmoid(c + s * (f - 0.5))
    fpad[:, 0:8] = f
    zero = jnp.zeros((8, 128), jnp.float32)
    rows = []
    for packed in (fpad[0:8] + pltpu.roll(fpad[8:16], 8, 1), fpad[16:24]):
        for bit in (1, 2, 4):
            packed = jnp.where(lax.rem(sub // bit, 2) == 1, pltpu.roll(packed, 128 - 16 * bit, 1), packed)
        packed = pltpu.roll(packed, me * 8, 1)
        rows.append(jnp.sum(packed, axis=0, keepdims=True))
    top, bottom = rows
    fsend[0:1, :] = top
    fsend[1:2, :] = bottom
    frecv[me, 0:1, :] = top
    frecv[me, 1:2, :] = bottom

    loads[2].wait()
    for r in range(8):
        for g in range(4):
            src1[4 + r, pl.ds(8 * g, 8), :] = tin[pl.ds(64 * g + r, 8, stride=8), :]

    pl.semaphore_wait(barrier, TRC + 1)

    def halo(buf, phase, side):
        return pltpu.make_async_remote_copy(
            src_ref=buf.at[pl.ds(4 + 4 * side, 4)],
            dst_ref=buf.at[pl.ds(12 - 12 * side, 4)],
            send_sem=hs_sem.at[phase, side],
            recv_sem=hr_sem.at[phase, side],
            device_id=((prev, after)[side], me),
            device_id_type=MESH,
        )

    def share(dest):
        return pltpu.make_async_remote_copy(
            src_ref=fsend, dst_ref=frecv.at[me], send_sem=fs_sem.at[dest], recv_sem=fr_sem.at[me],
            device_id=(tile, dest), device_id_type=MESH,
        )

    def spread(src, dst, s_sem, r_sem, dest):
        return pltpu.make_async_remote_copy(
            src_ref=src.at[dest], dst_ref=dst.at[me], send_sem=s_sem.at[dest], recv_sem=r_sem.at[me],
            device_id=(tile, dest), device_id_type=MESH,
        )

    def arrived(dst, r_sem, s_sem, source):
        return pltpu.make_async_remote_copy(
            src_ref=dst.at[source], dst_ref=dst.at[source], send_sem=s_sem.at[source],
            recv_sem=r_sem.at[source], device_id=(tile, source), device_id_type=MESH,
        )

    others = [lax.rem(me + k, TRC) for k in range(1, TRC)]
    for dest in others:
        share(dest).start()
    halo(src1, 0, 0).start()
    halo(src1, 0, 1).start()

    loads[4].wait()
    loads[5].wait()
    spot = lax.broadcasted_iota(jnp.int32, (32, 256), 1)
    j = lax.broadcasted_iota(jnp.int32, (32, 256), 0)
    at = lax.rem(j, 2) * 16 + j // 2
    rate = jnp.zeros((16, 256), jnp.float32)
    target = jnp.zeros((16, 256), jnp.float32)
    for p in range(2):
        place = (lax.rem(spot, 64) == at + 32 * p).astype(jnp.float32)
        rate += jnp.dot(kin[pl.ds(p, 16, stride=2), :], place, precision=EXACT, preferred_element_type=jnp.float32)
        target += jnp.dot(
            ctin[pl.ds(p, 16, stride=2), :].astype(jnp.float32), place, precision=EXACT,
            preferred_element_type=jnp.float32,
        )
    coarse = rate.astype(jnp.bfloat16).astype(jnp.float32)
    rate = jnp.where(lax.broadcasted_iota(jnp.int32, (16, 256), 1) < 128, coarse, rate - coarse)

    def fill(b, carry):
        hit = jnp.abs(target - b.astype(jnp.float32)) < 0.5
        abuf[b] = jnp.where(hit, rate, 0.0).astype(jnp.bfloat16)
        return carry

    lax.fori_loop(0, BINS, fill, 0)
    abuf[BINS] = rate.astype(jnp.bfloat16)

    loads[3].wait()
    for source in others:
        arrived(frecv, fr_sem, fs_sem, source).wait_recv()
    place = lax.rem(lane // 8 + 2 * sub, 16)
    spots = [place, lax.rem(place + 15, 16), place]
    frac = [zero, zero, zero]
    for source in range(TRC):
        rows = [jnp.broadcast_to(frecv[source, i : i + 1, :], (8, 128)) for i in (0, 0, 1)]
        frac = [jnp.where(spots[d] == source, rows[d], frac[d]) for d in range(3)]
    frac[1] = pltpu.roll(frac[1], 120, 1)
    weights = []
    for d in range(3):
        fd = pltpu.roll(frac[d], 0, 1, stride=16, stride_axis=0)
        weights.append(taps(fd, oin[8 * d : 8 * d + 8, :] == -1))
    cross, levels, along = weights
    upper = lax.rem(sub, 2) == 1
    level0 = levels[0] + levels[1] + jnp.where(upper, zero, levels[2])
    level1 = levels[3] + levels[4] + jnp.where(upper, levels[2], zero)
    for a in range(5):
        for level, lw in enumerate((level0, level1)):
            pair = cross[a] * lw
            for b in range(5):
                w = pair * along[b]
                if b != 2:
                    w = pltpu.roll(w, (b - 2) % 128, 1)
                wbuf[(b * 5 + a) * 2 + level] = w

    flags = (fl[tile], fl[after])
    mirror = 127 - lane

    def turn(buf, side):
        turned = jnp.full((8, 128), flags[side], jnp.int32) == 1

        def one(i, carry):
            for g in range(4):
                at = (12 * side + i, pl.ds(8 * g, 8), slice(None))
                v = buf[at]
                buf[at] = jnp.where(turned, jnp.take_along_axis(v, mirror, axis=1), v)
            return carry

        lax.fori_loop(0, 4, one, 0)

    def rims(buf, phase):
        for side in (1, 0):
            halo(buf, phase, side).wait_recv()
            turn(buf, 1 - side)

    rims(src1, 0)

    def first(x, carry):
        moved = transport(src1, wbuf, x)
        for l in range(2):
            for g in range(4):
                src2[4 + 2 * x + l, pl.ds(8 * g, 8), :] = moved[l][g]
        return carry

    lax.fori_loop(0, 2, first, 0)
    halo(src2, 1, 0).start()
    lax.fori_loop(2, 4, first, 0)
    halo(src2, 1, 1).start()
    rims(src2, 1)

    def second(k, carry):
        x = lax.rem(x_me + 1 + k, SIDE)
        moved = transport(src2, wbuf, x)
        for l in range(2):
            for g in range(2):
                even, odd = moved[l][g], moved[l][2 + g]
                at = pl.ds(8 * g, 8)
                send2[4 * x + 2 * l, at, :] = jnp.where(low, even, pltpu.roll(odd, 64, 1))
                send2[4 * x + 2 * l + 1, at, :] = jnp.where(low, pltpu.roll(even, 64, 1), odd)
        for i in range(1, SIDE):
            spread(send2, recv2, s2_sem, r2_sem, 4 * x + lax.rem(z_me + i, SIDE)).start()

        @pl.when(k < SIDE - 1)
        def _():
            spread(send2, recv2, s2_sem, r2_sem, 4 * x + z_me).start()

        return carry

    lax.fori_loop(0, SIDE, second, 0)
    recv2[me] = send2[me]
    for source in others:
        arrived(recv2, r2_sem, s2_sem, source).wait_recv()

    number = jnp.sum(jnp.abs(recv2[...]), axis=1)
    low16 = lax.broadcasted_iota(jnp.int32, (16, 128), 1) < 64
    other = pltpu.roll(number, 64, 1)
    none = jnp.zeros_like(number)
    nums = jnp.concatenate(
        [
            jnp.where(low16, number, none),
            jnp.where(low16, other, none),
            jnp.where(low16, none, other),
            jnp.where(low16, none, number),
        ],
        axis=0,
    )
    coarse = nums.astype(jnp.bfloat16)
    fine = (nums - coarse.astype(jnp.float32)).astype(jnp.bfloat16)
    nums = jnp.concatenate([coarse, fine, coarse, fine], axis=0)
    rates = jnp.dot(
        abuf[...].reshape((BINS + 1) * 16, 256), nums, preferred_element_type=jnp.float32
    )
    tbuf[...] = rates.reshape(BINS + 1, 16, 128)
    rbuf[...] = 1.0 / (1.0 + tbuf[BINS])

    def gain(k, carry):
        step = lax.rem(k + 1, TRC)
        g = lax.rem(x_me + step // SIDE, SIDE) * SIDE + lax.rem(z_me + step, SIDE)
        acc = [[None, None], [None, None]]
        for i in range(TRC):
            m = [recv2[i, 0:8, :], recv2[i, 8:16, :]]
            for p in range(2):
                t = jnp.broadcast_to(tbuf[2 * g + p, i : i + 1, :], (8, 128))
                for h in range(2):
                    term = t * m[h]
                    acc[p][h] = term if acc[p][h] is None else acc[p][h] + term
        rec = jnp.broadcast_to(rbuf[pl.ds(g, 1), :], (8, 128))
        for h in range(2):
            gained = jnp.where(low, acc[0][h], acc[1][h]) + pltpu.roll(jnp.where(low, acc[1][h], acc[0][h]), 64, 1)
            send3[g, 8 * h : 8 * h + 8, :] = (recv2[g, 8 * h : 8 * h + 8, :] + gained) * rec

        @pl.when(k < TRC - 1)
        def _():
            spread(send3, recv3, s3_sem, r3_sem, g).start()

        return carry

    lax.fori_loop(0, TRC, gain, 0)
    recv3[me] = send3[me]
    for source in others:
        arrived(recv3, r3_sem, s3_sem, source).wait_recv()
    for r in range(8):
        for h in range(2):
            c0, c1 = recv3[2 * r, 8 * h : 8 * h + 8, :], recv3[2 * r + 1, 8 * h : 8 * h + 8, :]
            out[pl.ds(64 * h + r, 8, stride=8), :] = jnp.where(low, c0, pltpu.roll(c1, 64, 1))
            out[pl.ds(128 + 64 * h + r, 8, stride=8), :] = jnp.where(low, pltpu.roll(c0, 64, 1), c1)

    for dest in others:
        share(dest).wait_send()
        spread(send2, recv2, s2_sem, r2_sem, dest).wait_send()
        spread(send3, recv3, s3_sem, r3_sem, dest).wait_send()
    for buf, phase in ((src1, 0), (src2, 1)):
        for side in range(2):
            halo(buf, phase, side).wait_send()


def solution(mesh):
    n_tile = mesh.shape["tile"]
    f32, i32, bf16 = jnp.float32, jnp.int32, jnp.bfloat16
    anywhere = pl.BlockSpec(memory_space=pltpu.HBM)

    def on_device(tracers, courant, shear, offsets, seam_flips, kernel, coag_target):
        result = pl.pallas_call(
            functools.partial(body, n_tile),
            out_shape=jax.ShapeDtypeStruct((256, 128), f32),
            in_specs=[anywhere] * 4 + [pl.BlockSpec(memory_space=pltpu.SMEM)] + [anywhere] * 2,
            out_specs=pl.BlockSpec(memory_space=pltpu.VMEM),
            scratch_shapes=[
                pltpu.VMEM((256, 128), f32),
                pltpu.VMEM((24, 8), f32),
                pltpu.VMEM((24, 8), f32),
                pltpu.VMEM((24, 128), i32),
                pltpu.VMEM((32, 32), f32),
                pltpu.VMEM((32, 32), i32),
                pltpu.VMEM((24, 128), f32),
                pltpu.VMEM((2, 128), f32),
                pltpu.VMEM((TRC, 2, 128), f32),
                pltpu.VMEM((50, 8, 128), f32),
                pltpu.VMEM((16, 32, 128), f32),
                pltpu.VMEM((16, 32, 128), f32),
                pltpu.VMEM((TRC, 16, 128), f32),
                pltpu.VMEM((TRC, 16, 128), f32),
                pltpu.VMEM((BINS + 1, 16, 256), bf16),
                pltpu.VMEM((64, 128), f32),
                pltpu.VMEM((BINS + 1, 16, 128), f32),
                pltpu.VMEM((16, 128), f32),
                pltpu.VMEM((TRC, 16, 128), f32),
                pltpu.VMEM((TRC, 16, 128), f32),
                pltpu.SemaphoreType.DMA((6,)),
                pltpu.SemaphoreType.DMA((2, 2)),
                pltpu.SemaphoreType.DMA((2, 2)),
                pltpu.SemaphoreType.DMA((TRC,)),
                pltpu.SemaphoreType.DMA((TRC,)),
                pltpu.SemaphoreType.DMA((TRC,)),
                pltpu.SemaphoreType.DMA((TRC,)),
                pltpu.SemaphoreType.DMA((TRC,)),
                pltpu.SemaphoreType.DMA((TRC,)),
            ],
            compiler_params=pltpu.CompilerParams(
                collective_id=0, has_side_effects=True, vmem_limit_bytes=48 * 1024 * 1024
            ),
        )(
            tracers.reshape(256, 128), courant.reshape(24, 8), shear.reshape(24, 8),
            offsets.reshape(24, 128), seam_flips, kernel, coag_target,
        )
        return result.reshape(32, 4, 2, 128)

    return jax.shard_map(
        on_device,
        mesh=mesh,
        in_specs=(
            P("trc", "tile", None, None),
            P(None, "tile", None, "trc"),
            P(None, "tile", None, "trc"),
            P(None, "tile", None, None),
            P(),
            P(),
            P(),
        ),
        out_specs=P("trc", "tile", None, None),
        check_vma=False,
    )
```

time: 146 us -> 45.3 us (0.31); the launches traced: 144 us -> 44.8 us
  blocking collectives: 79.6 us -> 0 us
  Pallas kernels: 0 us -> 39 us
  local copies, waits for them, and re-layouts: 25.3 us -> 5.77 us
  other arithmetic: 16.4 us -> 0 us
  starting transfers between devices: 16.4 us -> 0 us
  matrix products: 2.54 us -> 0 us
  between operations: 2.12 us -> 0.02 us
  waiting for transfers between devices: 1.54 us -> 0 us
    all_gather x1 -> x0, blocking collectives: 41.9 us -> none  [gather_turned(): lax.all_gather(both, axis, axis=0, tiled=True)]
    pallas_call x0 -> x1, Pallas kernels: none -> 39 us  [on_device(): pl.pallas_call(functools.partial(body, n_tile), out_shape=jax.ShapeDtypeS...]
    all_to_all x3 -> x0, blocking collectives: 37.7 us -> none  [the longest x2 19.5 us: moved_by_axis(): result = lax.all_to_all(result, axes[k], k, k, tiled=True)]
    ppermute x4 -> x0, starting transfers between devices: 16.4 us -> none  [the longest x2 12.6 us: with_halo(): lax.ppermute(head, axis, [((i + 1) % count, i) for i in range(count)])]
    slice x45 -> x0, local copies, waits for them, and re-layouts: 13.3 us -> none  [the longest x38 12.6 us: interpolate(): padded[:, x_step:x_step + cross, l_step:l_step + levels, y_step:y_step +...]
    add x2 -> x0, other arithmetic: 9.42 us -> none  [interpolate(): summed = summed + stencil[0, x_step] * stencil[1, l_step] * partial_sum]
    reshape x9 -> x0, local copies, waits for them, and re-layouts: 3.25 us -> none  [the longest x2 1.55 us: gather_turned(): both = jnp.concatenate([t.reshape(len(t), -1) for t in turned], axis=1)]
    all_to_all x3 -> x0, other arithmetic: 2.91 us -> none  [the longest x2 1.96 us: moved_by_axis(): result = lax.all_to_all(result, axes[k], k, k, tiled=True)]
  transfers between devices with their start and end apart: 4 -> 0, of which waited for: 1 -> 0; matrix products, arithmetic and copies ran while one was open for 3% -> 0% of each run, Pallas kernels for 0% -> 0%
where the time goes in v1:
time: 45.3 us; the launch traced here: 44.8 us
  Pallas kernels  39 us (86%)
  local copies, waits for them, and re-layouts  5.77 us (13%)
    pallas_call x1, Pallas kernels, on_device(): pl.pallas_call(functools.partial(body, n_tile), out_shape=jax.ShapeDtypeS...  39 us
    unnamed x15, local copies, waits for them, and re-layouts  5.77 us

profile of v1, /device:TPU:6, one launch (start us, length us, event | category | flops | bytes accessed | tf_op | source)
XLA Modules:
  0.0 44.8 jit_solution(16136510762509595641)
XLA Ops:
  0.0 0.0 copy-start.6
  0.0 0.7 %copy-done.6 = s32[32]{0:T(128)S(1)} copy-done((s32[32]{0:T(128)S(1)}, s32[32]{0:T(128)}, u32[]{:S(2)}) %copy-start.6) | copy-done | bytes 152
  0.7 0.0 copy-start
  0.7 0.9 %copy-done = f32[32,4,2,128]{3,2,1,0:T(2,128)S(1)} copy-done((f32[32,4,2,128]{3,2,1,0:T(2,128)S(1)}, f32[32,4,2,128]{3,2,1,0:T(2,128)}, u32[]{:S(2)}) %copy-start) | copy-done | bytes 131096
  1.6 0.0 copy-start.1
  1.6 0.7 %copy-done.1 = f32[32,32]{1,0:T(8,128)S(1)} copy-done((f32[32,32]{1,0:T(8,128)S(1)}, f32[32,32]{1,0:T(8,128)}, u32[]{:S(2)}) %copy-start.1) | copy-done | bytes 4120
  2.3 0.0 copy-start.2
  2.3 0.7 %copy-done.2 = s32[32,32]{1,0:T(8,128)S(1)} copy-done((s32[32,32]{1,0:T(8,128)S(1)}, s32[32,32]{1,0:T(8,128)}, u32[]{:S(2)}) %copy-start.2) | copy-done | bytes 4120
  3.0 0.0 copy-start.3
  3.0 0.7 %copy-done.3 = f32[3,4,2,8]{3,2,1,0:T(2,128)S(1)} copy-done((f32[3,4,2,8]{3,2,1,0:T(2,128)S(1)}, f32[3,4,2,8]{3,2,1,0:T(2,128)}, u32[]{:S(2)}) %copy-start.3) | copy-done | bytes 792
  3.7 0.0 copy-start.4
  3.7 0.7 %copy-done.4 = f32[3,4,2,8]{3,2,1,0:T(2,128)S(1)} copy-done((f32[3,4,2,8]{3,2,1,0:T(2,128)S(1)}, f32[3,4,2,8]{3,2,1,0:T(2,128)}, u32[]{:S(2)}) %copy-start.4) | copy-done | bytes 792
  4.4 0.0 copy-start.5
  4.4 0.7 %copy-done.5 = s32[3,4,2,128]{3,2,1,0:T(2,128)S(1)} copy-done((s32[3,4,2,128]{3,2,1,0:T(2,128)S(1)}, s32[3,4,2,128]{3,2,1,0:T(2,128)}, u32[]{:S(2)}) %copy-start.5) | copy-done | bytes 12312
  5.1 39.0 %shard_map.73 = f32[256,128]{1,0:T(8,128)S(1)} custom-call(f32[256,128]{1,0:T(8,128)S(1)} %bitcast.6, f32[24,8]{1,0:T(8,128)S(1)} %bitcast.7, f32[24,8]{1,0:T(8,128)S(1)} %bitcast.8, s32[24,128]{1,0:T(8,128)S(1)} %bitcast.9, s32[32]{0:T(128)S(1)} %copy-done.6, f32[32,32]{1,0:T(8,128)S(1)} %copy-done.1, s32[32,32]{1,0:T(8,128)S(1)} %copy-done.2), custom_call_target="tpu_custom_call" | custom-call | tf_op jit(solution)/shard_map/pallas_call | solution.py:324
  44.1 0.7 %copy.9 = f32[32,4,2,128]{3,2,1,0:T(2,128)} copy(f32[32,4,2,128]{3,2,1,0:T(2,128)S(1)} %bitcast.5) | data formatting | bytes 262144
Async XLA Ops:
  0.0 0.7 %copy-start.6 = (s32[32]{0:T(128)S(1)}, s32[32]{0:T(128)}, u32[]{:S(2)}) copy-start(s32[32]{0:T(128)} %fl.1) | copy-start | bytes 388
  0.7 0.9 %copy-start = (f32[32,4,2,128]{3,2,1,0:T(2,128)S(1)}, f32[32,4,2,128]{3,2,1,0:T(2,128)}, u32[]{:S(2)}) copy-start(f32[32,4,2,128]{3,2,1,0:T(2,128)} %param.7) | copy-start | bytes 393220
  1.6 0.7 %copy-start.1 = (f32[32,32]{1,0:T(8,128)S(1)}, f32[32,32]{1,0:T(8,128)}, u32[]{:S(2)}) copy-start(f32[32,32]{1,0:T(8,128)} %ke.1) | copy-start | bytes 12292
  2.3 0.7 %copy-start.2 = (s32[32,32]{1,0:T(8,128)S(1)}, s32[32,32]{1,0:T(8,128)}, u32[]{:S(2)}) copy-start(s32[32,32]{1,0:T(8,128)} %ct.1) | copy-start | bytes 12292
  3.0 0.7 %copy-start.3 = (f32[3,4,2,8]{3,2,1,0:T(2,128)S(1)}, f32[3,4,2,8]{3,2,1,0:T(2,128)}, u32[]{:S(2)}) copy-start(f32[3,4,2,8]{3,2,1,0:T(2,128)} %param.8) | copy-start | bytes 2308
  3.7 0.7 %copy-start.4 = (f32[3,4,2,8]{3,2,1,0:T(2,128)S(1)}, f32[3,4,2,8]{3,2,1,0:T(2,128)}, u32[]{:S(2)}) copy-start(f32[3,4,2,8]{3,2,1,0:T(2,128)} %param.9) | copy-start | bytes 2308
  4.4 0.7 %copy-start.5 = (s32[3,4,2,128]{3,2,1,0:T(2,128)S(1)}, s32[3,4,2,128]{3,2,1,0:T(2,128)}, u32[]{:S(2)}) copy-start(s32[3,4,2,128]{3,2,1,0:T(2,128)} %param.10) | copy-start | bytes 36868

commit v2 on v1

--- a/solution.py
+++ b/solution.py
@@ -51,8 +51,8 @@
 
 
 def body(
-    n_tile, tr, co, sh, of, fl, ke, ct, out,
-    tin, cin, sin, oin, kin, ctin, fpad, fsend, frecv, wbuf, src1, src2,
+    n_tile, tr, co, sh, of, fi, ke, ct, out,
+    tin, cin, sin, oin, fl, kin, ctin, fpad, fsend, frecv, wbuf, src1, src2,
     send2, recv2, abuf, nbuf, tbuf, rbuf, send3, recv3,
     in_sem, hs_sem, hr_sem, fs_sem, fr_sem, s2_sem, r2_sem, s3_sem, r3_sem,
 ):
@@ -64,7 +64,7 @@
     loads = [
         pltpu.make_async_copy(s, d, in_sem.at[i])
         for i, (s, d) in enumerate(
-            ((co, cin), (sh, sin), (tr, tin), (of, oin), (ke, kin), (ct, ctin))
+            ((co, cin), (sh, sin), (tr, tin), (of, oin), (ke, kin), (ct, ctin), (fi, fl))
         )
     ]
     for load in loads:
@@ -194,20 +194,18 @@
                     w = pltpu.roll(w, (b - 2) % 128, 1)
                 wbuf[(b * 5 + a) * 2 + level] = w
 
+    loads[6].wait()
     flags = (fl[tile], fl[after])
     mirror = 127 - lane
 
     def turn(buf, side):
         turned = jnp.full((8, 128), flags[side], jnp.int32) == 1
 
-        def one(i, carry):
+        for i in range(4):
             for g in range(4):
                 at = (12 * side + i, pl.ds(8 * g, 8), slice(None))
                 v = buf[at]
                 buf[at] = jnp.where(turned, jnp.take_along_axis(v, mirror, axis=1), v)
-            return carry
-
-        lax.fori_loop(0, 4, one, 0)
 
     def rims(buf, phase):
         for side in (1, 0):
@@ -229,8 +227,11 @@
     halo(src2, 1, 1).start()
     rims(src2, 1)
 
+    def plane(k):
+        return lax.rem(x_me + 6 - k + 3 * (k // 2) + 2 * (k // 3), SIDE)
+
     def second(k, carry):
-        x = lax.rem(x_me + 1 + k, SIDE)
+        x = plane(k)
         moved = transport(src2, wbuf, x)
         for l in range(2):
             for g in range(2):
@@ -238,7 +239,7 @@
                 at = pl.ds(8 * g, 8)
                 send2[4 * x + 2 * l, at, :] = jnp.where(low, even, pltpu.roll(odd, 64, 1))
                 send2[4 * x + 2 * l + 1, at, :] = jnp.where(low, pltpu.roll(even, 64, 1), odd)
-        for i in range(1, SIDE):
+        for i in (2, 1, 3):
             spread(send2, recv2, s2_sem, r2_sem, 4 * x + lax.rem(z_me + i, SIDE)).start()
 
         @pl.when(k < SIDE - 1)
@@ -275,28 +276,31 @@
     rbuf[...] = 1.0 / (1.0 + tbuf[BINS])
 
     def gain(k, carry):
-        step = lax.rem(k + 1, TRC)
-        g = lax.rem(x_me + step // SIDE, SIDE) * SIDE + lax.rem(z_me + step, SIDE)
-        acc = [[None, None], [None, None]]
+        x = plane(k)
+        acc = [[None] * 2 for _ in range(8)]
         for i in range(TRC):
             m = [recv2[i, 0:8, :], recv2[i, 8:16, :]]
-            for p in range(2):
-                t = jnp.broadcast_to(tbuf[2 * g + p, i : i + 1, :], (8, 128))
+            for b in range(8):
+                t = jnp.broadcast_to(tbuf[8 * x + b, i : i + 1, :], (8, 128))
                 for h in range(2):
                     term = t * m[h]
-                    acc[p][h] = term if acc[p][h] is None else acc[p][h] + term
-        rec = jnp.broadcast_to(rbuf[pl.ds(g, 1), :], (8, 128))
-        for h in range(2):
-            gained = jnp.where(low, acc[0][h], acc[1][h]) + pltpu.roll(jnp.where(low, acc[1][h], acc[0][h]), 64, 1)
-            send3[g, 8 * h : 8 * h + 8, :] = (recv2[g, 8 * h : 8 * h + 8, :] + gained) * rec
-
-        @pl.when(k < TRC - 1)
-        def _():
-            spread(send3, recv3, s3_sem, r3_sem, g).start()
+                    acc[b][h] = term if acc[b][h] is None else acc[b][h] + term
+        for z in range(SIDE):
+            g = 4 * x + z
+            rec = jnp.broadcast_to(rbuf[pl.ds(g, 1), :], (8, 128))
+            for h in range(2):
+                even, odd = acc[2 * z][h], acc[2 * z + 1][h]
+                gained = jnp.where(low, even, odd) + pltpu.roll(jnp.where(low, odd, even), 64, 1)
+                send3[g, 8 * h : 8 * h + 8, :] = (recv2[g, 8 * h : 8 * h + 8, :] + gained) * rec
+        for z in range(SIDE):
+
+            @pl.when(4 * x + z != me)
+            def _(z=z):
+                spread(send3, recv3, s3_sem, r3_sem, 4 * x + z).start()
 
         return carry
 
-    lax.fori_loop(0, TRC, gain, 0)
+    lax.fori_loop(0, SIDE, gain, 0)
     recv3[me] = send3[me]
     for source in others:
         arrived(recv3, r3_sem, s3_sem, source).wait_recv()
@@ -324,13 +328,14 @@
         result = pl.pallas_call(
             functools.partial(body, n_tile),
             out_shape=jax.ShapeDtypeStruct((256, 128), f32),
-            in_specs=[anywhere] * 4 + [pl.BlockSpec(memory_space=pltpu.SMEM)] + [anywhere] * 2,
+            in_specs=[anywhere] * 7,
             out_specs=pl.BlockSpec(memory_space=pltpu.VMEM),
             scratch_shapes=[
                 pltpu.VMEM((256, 128), f32),
                 pltpu.VMEM((24, 8), f32),
                 pltpu.VMEM((24, 8), f32),
                 pltpu.VMEM((24, 128), i32),
+                pltpu.SMEM((32,), i32),
                 pltpu.VMEM((32, 32), f32),
                 pltpu.VMEM((32, 32), i32),
                 pltpu.VMEM((24, 128), f32),
@@ -347,7 +352,7 @@
                 pltpu.VMEM((16, 128), f32),
                 pltpu.VMEM((TRC, 16, 128), f32),
                 pltpu.VMEM((TRC, 16, 128), f32),
-                pltpu.SemaphoreType.DMA((6,)),
+                pltpu.SemaphoreType.DMA((7,)),
                 pltpu.SemaphoreType.DMA((2, 2)),
                 pltpu.SemaphoreType.DMA((2, 2)),
                 pltpu.SemaphoreType.DMA((TRC,)),
@@ -361,8 +366,13 @@
                 collective_id=0, has_side_effects=True, vmem_limit_bytes=48 * 1024 * 1024
             ),
         )(
-            tracers.reshape(256, 128), courant.reshape(24, 8), shear.reshape(24, 8),
-            offsets.reshape(24, 128), seam_flips, kernel, coag_target,
+            *(
+                pltpu.with_memory_space_constraint(v, pltpu.HBM)
+                for v in (
+                    tracers.reshape(256, 128), courant.reshape(24, 8), shear.reshape(24, 8),
+                    offsets.reshape(24, 128), seam_flips, kernel, coag_target,
+                )
+            ),
         )
         return result.reshape(32, 4, 2, 128)
 

time: 45.3 us -> 37.7 us (0.83)
  local copies, waits for them, and re-layouts: 5.77 us -> 0.66 us
  Pallas kernels: 39 us -> 36.8 us
    unnamed x15 -> x1, local copies, waits for them, and re-layouts: 5.77 us -> 0.66 us
    pallas_call x1, Pallas kernels: 39 us -> 36.8 us  [on_device(): pl.pallas_call(functools.partial(body, n_tile), out_shape=jax.ShapeDtypeS...]
where the time goes in v2:
time: 37.7 us; the launch traced here: 37.5 us
  Pallas kernels  36.8 us (98%)
  local copies, waits for them, and re-layouts  0.66 us (2%)
    pallas_call x1, Pallas kernels, on_device(): pl.pallas_call(functools.partial(body, n_tile), out_shape=jax.ShapeDtypeS...  36.8 us

profile of v2, /device:TPU:6, one launch (start us, length us, event | category | flops | bytes accessed | tf_op | source)
XLA Modules:
  0.0 37.5 jit_solution(13953025562671155296)
XLA Ops:
  0.0 36.8 %shard_map.73 = f32[256,128]{1,0:T(8,128)S(1)} custom-call(f32[256,128]{1,0:T(8,128)} %bitcast.6, f32[24,8]{1,0:T(8,128)} %bitcast.7, f32[24,8]{1,0:T(8,128)} %bitcast.8, s32[24,128]{1,0:T(8,128)} %bitcast.9, s32[32]{0:T(128)} %fi.1, f32[32,32]{1,0:T(8,128)} %ke.1, s32[32,32]{1,0:T(8,128)} %ct.1), custom_call_target="tpu_custom_call" | custom-call | tf_op jit(solution)/shard_map/pallas_call | solution.py:328
  36.9 0.7 %copy.9 = f32[32,4,2,128]{3,2,1,0:T(2,128)} copy(f32[32,4,2,128]{3,2,1,0:T(2,128)S(1)} %bitcast.5) | data formatting | bytes 262144

commit v3 on v2

--- a/solution.py
+++ b/solution.py
@@ -61,6 +61,20 @@
     prev = lax.rem(tile + n_tile - 1, n_tile)
     after = lax.rem(tile + 1, n_tile)
 
+    quad = lax.rem(tile, 4)
+    side_far = lax.rem(quad, 2)
+    partner = tile + 2 - 4 * (quad // 2)
+
+    def plane(k):
+        return lax.rem(x_me + 6 - k + 3 * (k // 2) + 2 * (k // 3), SIDE)
+
+    others = [4 * plane(k) + lax.rem(z_me + i, SIDE) for k in range(SIDE) for i in (2, 1, 3, 0)][:-1]
+    barrier = pltpu.get_barrier_semaphore()
+    for dest in others:
+        pl.semaphore_signal(barrier, inc=1, device_id=(tile, dest), device_id_type=MESH)
+    for t in (prev, after):
+        pl.semaphore_signal(barrier, inc=1, device_id=(t, me), device_id_type=MESH)
+
     loads = [
         pltpu.make_async_copy(s, d, in_sem.at[i])
         for i, (s, d) in enumerate(
@@ -69,12 +83,9 @@
     ]
     for load in loads:
         load.start()
-
-    barrier = pltpu.get_barrier_semaphore()
-    for k in range(1, TRC):
-        pl.semaphore_signal(barrier, inc=1, device_id=(tile, lax.rem(me + k, TRC)), device_id_type=MESH)
-    for t in (prev, after):
-        pl.semaphore_signal(barrier, inc=1, device_id=(t, me), device_id_type=MESH)
+    for k in range(TRC):
+        dest = lax.rem(me + k, TRC)
+        pl.semaphore_signal(barrier, inc=1, device_id=(partner, dest), device_id_type=MESH)
 
     lane = lax.broadcasted_iota(jnp.int32, (8, 128), 1)
     sub = lax.broadcasted_iota(jnp.int32, (8, 128), 0)
@@ -106,15 +117,25 @@
         for g in range(4):
             src1[4 + r, pl.ds(8 * g, 8), :] = tin[pl.ds(64 * g + r, 8, stride=8), :]
 
-    pl.semaphore_wait(barrier, TRC + 1)
-
-    def halo(buf, phase, side):
+    pl.semaphore_wait(barrier, 2 * TRC + 1)
+
+    def halo(side):
         return pltpu.make_async_remote_copy(
-            src_ref=buf.at[pl.ds(4 + 4 * side, 4)],
-            dst_ref=buf.at[pl.ds(12 - 12 * side, 4)],
-            send_sem=hs_sem.at[phase, side],
-            recv_sem=hr_sem.at[phase, side],
+            src_ref=src1.at[pl.ds(4 + 4 * side, 4)],
+            dst_ref=src1.at[pl.ds(12 - 12 * side, 4)],
+            send_sem=hs_sem.at[0, side],
+            recv_sem=hr_sem.at[0, side],
             device_id=((prev, after)[side], me),
+            device_id_type=MESH,
+        )
+
+    def moved_halo(side, i):
+        return pltpu.make_async_remote_copy(
+            src_ref=src2.at[pl.ds(4 + 4 * side + 2 * i, 2)],
+            dst_ref=src2.at[pl.ds(12 - 12 * side + 2 * i, 2)],
+            send_sem=hs_sem.at[1 + i, side],
+            recv_sem=hr_sem.at[1 + i, side],
+            device_id=(lax.rem(tile + n_tile - 1 + 2 * side, n_tile), me),
             device_id_type=MESH,
         )
 
@@ -127,7 +148,7 @@
     def spread(src, dst, s_sem, r_sem, dest):
         return pltpu.make_async_remote_copy(
             src_ref=src.at[dest], dst_ref=dst.at[me], send_sem=s_sem.at[dest], recv_sem=r_sem.at[me],
-            device_id=(tile, dest), device_id_type=MESH,
+            device_id=(partner, dest), device_id_type=MESH,
         )
 
     def arrived(dst, r_sem, s_sem, source):
@@ -136,11 +157,10 @@
             recv_sem=r_sem.at[source], device_id=(tile, source), device_id_type=MESH,
         )
 
-    others = [lax.rem(me + k, TRC) for k in range(1, TRC)]
     for dest in others:
         share(dest).start()
-    halo(src1, 0, 0).start()
-    halo(src1, 0, 1).start()
+    halo(0).start()
+    halo(1).start()
 
     loads[4].wait()
     loads[5].wait()
@@ -166,6 +186,21 @@
 
     lax.fori_loop(0, BINS, fill, 0)
     abuf[BINS] = rate.astype(jnp.bfloat16)
+
+    mirror = 127 - lane
+    loads[6].wait()
+
+    def turn(buf, side):
+        turned = jnp.full((8, 128), fl[lax.rem(tile + side, n_tile)], jnp.int32) == 1
+        for i in range(4):
+            for g in range(4):
+                at = (12 * side + i, pl.ds(8 * g, 8), slice(None))
+                v = buf[at]
+                buf[at] = jnp.where(turned, jnp.take_along_axis(v, mirror, axis=1), v)
+
+    for side in range(2):
+        halo(1 - side).wait_recv()
+        turn(src1, side)
 
     loads[3].wait()
     for source in others:
@@ -194,44 +229,27 @@
                     w = pltpu.roll(w, (b - 2) % 128, 1)
                 wbuf[(b * 5 + a) * 2 + level] = w
 
-    loads[6].wait()
-    flags = (fl[tile], fl[after])
-    mirror = 127 - lane
-
-    def turn(buf, side):
-        turned = jnp.full((8, 128), flags[side], jnp.int32) == 1
-
-        for i in range(4):
-            for g in range(4):
-                at = (12 * side + i, pl.ds(8 * g, 8), slice(None))
-                v = buf[at]
-                buf[at] = jnp.where(turned, jnp.take_along_axis(v, mirror, axis=1), v)
-
-    def rims(buf, phase):
-        for side in (1, 0):
-            halo(buf, phase, side).wait_recv()
-            turn(buf, 1 - side)
-
-    rims(src1, 0)
-
-    def first(x, carry):
+    def first(k, carry):
+        side = lax.rem(side_far + k // 2, 2)
+        x = 2 * side + lax.rem(k, 2)
         moved = transport(src1, wbuf, x)
         for l in range(2):
             for g in range(4):
                 src2[4 + 2 * x + l, pl.ds(8 * g, 8), :] = moved[l][g]
+        moved_halo(side, lax.rem(k, 2)).start()
         return carry
 
-    lax.fori_loop(0, 2, first, 0)
-    halo(src2, 1, 0).start()
-    lax.fori_loop(2, 4, first, 0)
-    halo(src2, 1, 1).start()
-    rims(src2, 1)
-
-    def plane(k):
-        return lax.rem(x_me + 6 - k + 3 * (k // 2) + 2 * (k // 3), SIDE)
+    lax.fori_loop(0, 4, first, 0)
+
+    def rim(side):
+        for i in range(2):
+            moved_halo(1 - side, i).wait_recv()
+        turn(src2, side)
 
     def second(k, carry):
-        x = plane(k)
+        pair = 2 * lax.rem(1 - side_far + k // 2, 2)
+        near = lax.rem(x_me + 5 - pair, SIDE) // 2
+        x = pair + lax.rem(1 - near + k, 2)
         moved = transport(src2, wbuf, x)
         for l in range(2):
             for g in range(2):
@@ -239,21 +257,21 @@
                 at = pl.ds(8 * g, 8)
                 send2[4 * x + 2 * l, at, :] = jnp.where(low, even, pltpu.roll(odd, 64, 1))
                 send2[4 * x + 2 * l + 1, at, :] = jnp.where(low, pltpu.roll(even, 64, 1), odd)
-        for i in (2, 1, 3):
-            spread(send2, recv2, s2_sem, r2_sem, 4 * x + lax.rem(z_me + i, SIDE)).start()
-
-        @pl.when(k < SIDE - 1)
-        def _():
-            spread(send2, recv2, s2_sem, r2_sem, 4 * x + z_me).start()
-
+        for i in range(SIDE):
+            spread(send2, recv2, s2_sem, r2_sem, 4 * x + zs[i]).start()
         return carry
 
-    lax.fori_loop(0, SIDE, second, 0)
-    recv2[me] = send2[me]
-    for source in others:
+    zs = [lax.rem(z_me + 1 + quad // 2 + i, SIDE) for i in range(SIDE)]
+    rim(1 - side_far)
+    lax.fori_loop(0, 2, second, 0)
+    rim(side_far)
+    lax.fori_loop(2, 4, second, 0)
+
+    sources = [4 * plane(k) + lax.rem(z_me + quad // 2 + 3 + i, SIDE) for k in (3, 2, 1, 0) for i in range(SIDE)]
+    for source in sources:
         arrived(recv2, r2_sem, s2_sem, source).wait_recv()
-
-    number = jnp.sum(jnp.abs(recv2[...]), axis=1)
+        nbuf[pl.ds(source, 1), :] = jnp.sum(jnp.abs(recv2[source]), axis=0, keepdims=True)
+    number = nbuf[...]
     low16 = lax.broadcasted_iota(jnp.int32, (16, 128), 1) < 64
     other = pltpu.roll(number, 64, 1)
     none = jnp.zeros_like(number)
@@ -292,31 +310,31 @@
                 even, odd = acc[2 * z][h], acc[2 * z + 1][h]
                 gained = jnp.where(low, even, odd) + pltpu.roll(jnp.where(low, odd, even), 64, 1)
                 send3[g, 8 * h : 8 * h + 8, :] = (recv2[g, 8 * h : 8 * h + 8, :] + gained) * rec
+        for i in range(SIDE):
+            spread(send3, recv3, s3_sem, r3_sem, 4 * x + zs[i]).start()
+        return carry
+
+    lax.fori_loop(0, SIDE, gain, 0)
+    for k in (3, 2, 1, 0):
+        x = plane(k)
         for z in range(SIDE):
-
-            @pl.when(4 * x + z != me)
-            def _(z=z):
-                spread(send3, recv3, s3_sem, r3_sem, 4 * x + z).start()
-
-        return carry
-
-    lax.fori_loop(0, SIDE, gain, 0)
-    recv3[me] = send3[me]
-    for source in others:
-        arrived(recv3, r3_sem, s3_sem, source).wait_recv()
-    for r in range(8):
-        for h in range(2):
-            c0, c1 = recv3[2 * r, 8 * h : 8 * h + 8, :], recv3[2 * r + 1, 8 * h : 8 * h + 8, :]
-            out[pl.ds(64 * h + r, 8, stride=8), :] = jnp.where(low, c0, pltpu.roll(c1, 64, 1))
-            out[pl.ds(128 + 64 * h + r, 8, stride=8), :] = jnp.where(low, pltpu.roll(c0, 64, 1), c1)
+            arrived(recv3, r3_sem, s3_sem, 4 * x + z).wait_recv()
+        for i in range(2):
+            r = 2 * x + i
+            for h in range(2):
+                c0, c1 = recv3[2 * r, 8 * h : 8 * h + 8, :], recv3[2 * r + 1, 8 * h : 8 * h + 8, :]
+                out[pl.ds(64 * h + r, 8, stride=8), :] = jnp.where(low, c0, pltpu.roll(c1, 64, 1))
+                out[pl.ds(128 + 64 * h + r, 8, stride=8), :] = jnp.where(low, pltpu.roll(c0, 64, 1), c1)
 
     for dest in others:
         share(dest).wait_send()
+    for dest in range(TRC):
         spread(send2, recv2, s2_sem, r2_sem, dest).wait_send()
         spread(send3, recv3, s3_sem, r3_sem, dest).wait_send()
-    for buf, phase in ((src1, 0), (src2, 1)):
-        for side in range(2):
-            halo(buf, phase, side).wait_send()
+    for side in range(2):
+        halo(side).wait_send()
+        for i in range(2):
+            moved_halo(side, i).wait_send()
 
 
 def solution(mesh):
@@ -347,14 +365,14 @@
                 pltpu.VMEM((TRC, 16, 128), f32),
                 pltpu.VMEM((TRC, 16, 128), f32),
                 pltpu.VMEM((BINS + 1, 16, 256), bf16),
-                pltpu.VMEM((64, 128), f32),
+                pltpu.VMEM((16, 128), f32),
                 pltpu.VMEM((BINS + 1, 16, 128), f32),
                 pltpu.VMEM((16, 128), f32),
                 pltpu.VMEM((TRC, 16, 128), f32),
                 pltpu.VMEM((TRC, 16, 128), f32),
                 pltpu.SemaphoreType.DMA((7,)),
-                pltpu.SemaphoreType.DMA((2, 2)),
-                pltpu.SemaphoreType.DMA((2, 2)),
+                pltpu.SemaphoreType.DMA((3, 2)),
+                pltpu.SemaphoreType.DMA((3, 2)),
                 pltpu.SemaphoreType.DMA((TRC,)),
                 pltpu.SemaphoreType.DMA((TRC,)),
                 pltpu.SemaphoreType.DMA((TRC,)),

time: 37.7 us -> 37.1 us (0.984)
  Pallas kernels: 36.8 us -> 36.2 us
    pallas_call x1, Pallas kernels: 36.8 us -> 36.2 us  [on_device(): pl.pallas_call(functools.partial(body, n_tile), out_shape=jax.ShapeDtypeS...]
where the time goes in v3:
time: 37.1 us; the launch traced here: 36.9 us
  Pallas kernels  36.2 us (98%)
  local copies, waits for them, and re-layouts  0.66 us (2%)
    pallas_call x1, Pallas kernels, on_device(): pl.pallas_call(functools.partial(body, n_tile), out_shape=jax.ShapeDtypeS...  36.2 us

profile of v3, /device:TPU:6, one launch (start us, length us, event | category | flops | bytes accessed | tf_op | source)
XLA Modules:
  0.0 36.9 jit_solution(16737483302029280924)
XLA Ops:
  0.0 36.2 %shard_map.73 = f32[256,128]{1,0:T(8,128)S(1)} custom-call(f32[256,128]{1,0:T(8,128)} %bitcast.6, f32[24,8]{1,0:T(8,128)} %bitcast.7, f32[24,8]{1,0:T(8,128)} %bitcast.8, s32[24,128]{1,0:T(8,128)} %bitcast.9, s32[32]{0:T(128)} %fi.1, f32[32,32]{1,0:T(8,128)} %ke.1, s32[32,32]{1,0:T(8,128)} %ct.1), custom_call_target="tpu_custom_call" | custom-call | tf_op jit(solution)/shard_map/pallas_call | solution.py:346
  36.3 0.7 %copy.9 = f32[32,4,2,128]{3,2,1,0:T(2,128)} copy(f32[32,4,2,128]{3,2,1,0:T(2,128)S(1)} %bitcast.5) | data formatting | bytes 262144

commit v4 on v3

--- a/solution.py
+++ b/solution.py
@@ -31,11 +31,10 @@
     ]
 
 
-def transport(src, wbuf, x):
-    out = None
+def transport(src, wbuf, x, steps=range(5), out=None):
     for b in range(5):
         acc = [[None] * 4, [None] * 4]
-        for a in range(5):
+        for a in steps:
             for level in range(2):
                 q = [src[2 * x + 2 * a + level, pl.ds(8 * g, 8), :] for g in range(4)]
                 for l in range(2):
@@ -52,9 +51,9 @@
 
 def body(
     n_tile, tr, co, sh, of, fi, ke, ct, out,
-    tin, cin, sin, oin, fl, kin, ctin, fpad, fsend, frecv, wbuf, src1, src2,
+    tin, cin, sin, oin, fl, kin, ctin, fpad, fsend, frecv, wbuf, src1, src2, part,
     send2, recv2, abuf, nbuf, tbuf, rbuf, send3, recv3,
-    in_sem, hs_sem, hr_sem, fs_sem, fr_sem, s2_sem, r2_sem, s3_sem, r3_sem,
+    in_sem, hs_sem, hr_sem, fs_sem, fr_sem, known_sem, s2_sem, r2_sem, s3_sem, r3_sem,
 ):
     tile, me = lax.axis_index("tile"), lax.axis_index("trc")
     x_me, z_me = me // SIDE, lax.rem(me, SIDE)
@@ -83,9 +82,6 @@
     ]
     for load in loads:
         load.start()
-    for k in range(TRC):
-        dest = lax.rem(me + k, TRC)
-        pl.semaphore_signal(barrier, inc=1, device_id=(partner, dest), device_id_type=MESH)
 
     lane = lax.broadcasted_iota(jnp.int32, (8, 128), 1)
     sub = lax.broadcasted_iota(jnp.int32, (8, 128), 0)
@@ -117,7 +113,7 @@
         for g in range(4):
             src1[4 + r, pl.ds(8 * g, 8), :] = tin[pl.ds(64 * g + r, 8, stride=8), :]
 
-    pl.semaphore_wait(barrier, 2 * TRC + 1)
+    pl.semaphore_wait(barrier, TRC + 1)
 
     def halo(side):
         return pltpu.make_async_remote_copy(
@@ -157,8 +153,14 @@
             recv_sem=r_sem.at[source], device_id=(tile, source), device_id_type=MESH,
         )
 
-    for dest in others:
-        share(dest).start()
+    for z in (3, 2, 1, 0):
+        for i in (2, 1, 3, 0):
+            dest = 4 * lax.rem(x_me + i, SIDE) + z
+
+            @pl.when(dest != me)
+            def _(dest=dest):
+                share(dest).start()
+
     halo(0).start()
     halo(1).start()
 
@@ -181,11 +183,11 @@
 
     def fill(b, carry):
         hit = jnp.abs(target - b.astype(jnp.float32)) < 0.5
-        abuf[b] = jnp.where(hit, rate, 0.0).astype(jnp.bfloat16)
+        abuf[1 + 8 * (lax.rem(b, 8) // 2) + 2 * (b // 8) + lax.rem(b, 2)] = jnp.where(hit, rate, 0.0).astype(jnp.bfloat16)
         return carry
 
     lax.fori_loop(0, BINS, fill, 0)
-    abuf[BINS] = rate.astype(jnp.bfloat16)
+    abuf[0] = rate.astype(jnp.bfloat16)
 
     mirror = 127 - lane
     loads[6].wait()
@@ -205,6 +207,15 @@
     loads[3].wait()
     for source in others:
         arrived(frecv, fr_sem, fs_sem, source).wait_recv()
+
+    inner = (quad + 1) // 2 == 1
+
+    @pl.when(inner)
+    def _():
+        pl.semaphore_signal(
+            known_sem, inc=1, device_id=(lax.rem(tile + n_tile - 1 + 2 * side_far, n_tile), me), device_id_type=MESH
+        )
+
     place = lax.rem(lane // 8 + 2 * sub, 16)
     spots = [place, lax.rem(place + 15, 16), place]
     frac = [zero, zero, zero]
@@ -246,31 +257,59 @@
             moved_halo(1 - side, i).wait_recv()
         turn(src2, side)
 
-    def second(k, carry):
-        pair = 2 * lax.rem(1 - side_far + k // 2, 2)
-        near = lax.rem(x_me + 5 - pair, SIDE) // 2
-        x = pair + lax.rem(1 - near + k, 2)
-        moved = transport(src2, wbuf, x)
+    zs = [lax.rem(z_me + 1 + quad // 2 + i, SIDE) for i in range(SIDE)]
+
+    def pack(moved, x):
         for l in range(2):
             for g in range(2):
                 even, odd = moved[l][g], moved[l][2 + g]
                 at = pl.ds(8 * g, 8)
                 send2[4 * x + 2 * l, at, :] = jnp.where(low, even, pltpu.roll(odd, 64, 1))
                 send2[4 * x + 2 * l + 1, at, :] = jnp.where(low, pltpu.roll(even, 64, 1), odd)
-        for i in range(SIDE):
-            spread(send2, recv2, s2_sem, r2_sem, 4 * x + zs[i]).start()
+
+    def leave(side):
+        near = lax.rem(x_me + 5 - 2 * side, SIDE) // 2
+        for k in range(2):
+            x = 2 * side + lax.rem(1 - near + k, 2)
+            for i in range(SIDE):
+                spread(send2, recv2, s2_sem, r2_sem, 4 * x + zs[i]).start()
+
+    def early(k, carry):
+        x = 2 * (1 - side_far) + k
+        pack(transport(src2, wbuf, x), x)
         return carry
 
-    zs = [lax.rem(z_me + 1 + quad // 2 + i, SIDE) for i in range(SIDE)]
     rim(1 - side_far)
-    lax.fori_loop(0, 2, second, 0)
-    rim(side_far)
-    lax.fori_loop(2, 4, second, 0)
+    lax.fori_loop(0, 2, early, 0)
+
+    steps = [4 * side_far + n * (1 - 2 * side_far) for n in range(5)]
+    cells = ((3 * side_far, 2), (1 + side_far, 1))
+    for i, (x, reach) in enumerate(cells):
+        moved = transport(src2, wbuf, x, steps[reach:])
+        for l in range(2):
+            for g in range(4):
+                part[2 * i + l, pl.ds(8 * g, 8), :] = moved[l][g]
+
+    @pl.when(inner)
+    def _():
+        pl.semaphore_wait(known_sem, 1)
+
+    for i in range(2):
+        moved_halo(1 - side_far, i).wait_recv()
+    leave(1 - side_far)
+    turn(src2, side_far)
+    for i, (x, reach) in enumerate(cells):
+        moved = [[part[2 * i + l, pl.ds(8 * g, 8), :] for g in range(4)] for l in range(2)]
+        pack(transport(src2, wbuf, x, steps[:reach], moved), x)
+    leave(side_far)
 
     sources = [4 * plane(k) + lax.rem(z_me + quad // 2 + 3 + i, SIDE) for k in (3, 2, 1, 0) for i in range(SIDE)]
-    for source in sources:
-        arrived(recv2, r2_sem, s2_sem, source).wait_recv()
-        nbuf[pl.ds(source, 1), :] = jnp.sum(jnp.abs(recv2[source]), axis=0, keepdims=True)
+    for k in range(SIDE):
+        group = sources[SIDE * k : SIDE * k + SIDE]
+        for source in group:
+            arrived(recv2, r2_sem, s2_sem, source).wait_recv()
+        for source in group:
+            nbuf[pl.ds(source, 1), :] = jnp.sum(jnp.abs(recv2[source]), axis=0, keepdims=True)
     number = nbuf[...]
     low16 = lax.broadcasted_iota(jnp.int32, (16, 128), 1) < 64
     other = pltpu.roll(number, 64, 1)
@@ -287,34 +326,49 @@
     coarse = nums.astype(jnp.bfloat16)
     fine = (nums - coarse.astype(jnp.float32)).astype(jnp.bfloat16)
     nums = jnp.concatenate([coarse, fine, coarse, fine], axis=0)
-    rates = jnp.dot(
-        abuf[...].reshape((BINS + 1) * 16, 256), nums, preferred_element_type=jnp.float32
-    )
-    tbuf[...] = rates.reshape(BINS + 1, 16, 128)
-    rbuf[...] = 1.0 / (1.0 + tbuf[BINS])
-
-    def gain(k, carry):
-        x = plane(k)
+
+    def rates(start, count):
+        found = jnp.dot(
+            abuf[start : start + count].reshape(count * 16, 256), nums, preferred_element_type=jnp.float32
+        )
+        tbuf[start : start + count] = found.reshape(count, 16, 128)
+
+    def gain(z):
         acc = [[None] * 2 for _ in range(8)]
         for i in range(TRC):
             m = [recv2[i, 0:8, :], recv2[i, 8:16, :]]
             for b in range(8):
-                t = jnp.broadcast_to(tbuf[8 * x + b, i : i + 1, :], (8, 128))
+                t = jnp.broadcast_to(tbuf[1 + 8 * z + b, i : i + 1, :], (8, 128))
                 for h in range(2):
                     term = t * m[h]
                     acc[b][h] = term if acc[b][h] is None else acc[b][h] + term
-        for z in range(SIDE):
+        for x in range(SIDE):
             g = 4 * x + z
-            rec = jnp.broadcast_to(rbuf[pl.ds(g, 1), :], (8, 128))
+            rec = jnp.broadcast_to(rbuf[g : g + 1, :], (8, 128))
             for h in range(2):
-                even, odd = acc[2 * z][h], acc[2 * z + 1][h]
+                even, odd = acc[2 * x][h], acc[2 * x + 1][h]
                 gained = jnp.where(low, even, odd) + pltpu.roll(jnp.where(low, odd, even), 64, 1)
                 send3[g, 8 * h : 8 * h + 8, :] = (recv2[g, 8 * h : 8 * h + 8, :] + gained) * rec
-        for i in range(SIDE):
-            spread(send3, recv3, s3_sem, r3_sem, 4 * x + zs[i]).start()
-        return carry
-
-    lax.fori_loop(0, SIDE, gain, 0)
+        for i in (2, 1, 3, 0):
+            spread(send3, recv3, s3_sem, r3_sem, 4 * lax.rem(x_me + i, SIDE) + z).start()
+
+    rates(0, 9)
+    rbuf[...] = 1.0 / (1.0 + tbuf[0])
+    for z in range(SIDE):
+        if z < SIDE - 1:
+            rates(9 + 8 * z, 8)
+        gain(z)
+
+    for dest in others:
+        share(dest).wait_send()
+    for side in range(2):
+        halo(side).wait_send()
+        for i in range(2):
+            moved_halo(side, i).wait_send()
+    for dest in range(TRC):
+        spread(send2, recv2, s2_sem, r2_sem, dest).wait_send()
+    for dest in range(TRC):
+        spread(send3, recv3, s3_sem, r3_sem, dest).wait_send()
     for k in (3, 2, 1, 0):
         x = plane(k)
         for z in range(SIDE):
@@ -325,16 +379,6 @@
                 c0, c1 = recv3[2 * r, 8 * h : 8 * h + 8, :], recv3[2 * r + 1, 8 * h : 8 * h + 8, :]
                 out[pl.ds(64 * h + r, 8, stride=8), :] = jnp.where(low, c0, pltpu.roll(c1, 64, 1))
                 out[pl.ds(128 + 64 * h + r, 8, stride=8), :] = jnp.where(low, pltpu.roll(c0, 64, 1), c1)
-
-    for dest in others:
-        share(dest).wait_send()
-    for dest in range(TRC):
-        spread(send2, recv2, s2_sem, r2_sem, dest).wait_send()
-        spread(send3, recv3, s3_sem, r3_sem, dest).wait_send()
-    for side in range(2):
-        halo(side).wait_send()
-        for i in range(2):
-            moved_halo(side, i).wait_send()
 
 
 def solution(mesh):
@@ -362,6 +406,7 @@
                 pltpu.VMEM((50, 8, 128), f32),
                 pltpu.VMEM((16, 32, 128), f32),
                 pltpu.VMEM((16, 32, 128), f32),
+                pltpu.VMEM((4, 32, 128), f32),
                 pltpu.VMEM((TRC, 16, 128), f32),
                 pltpu.VMEM((TRC, 16, 128), f32),
                 pltpu.VMEM((BINS + 1, 16, 256), bf16),
@@ -375,6 +420,7 @@
                 pltpu.SemaphoreType.DMA((3, 2)),
                 pltpu.SemaphoreType.DMA((TRC,)),
                 pltpu.SemaphoreType.DMA((TRC,)),
+                pltpu.SemaphoreType.REGULAR,
                 pltpu.SemaphoreType.DMA((TRC,)),
                 pltpu.SemaphoreType.DMA((TRC,)),
                 pltpu.SemaphoreType.DMA((TRC,)),

time: 37.1 us -> 36.1 us (0.973)
  Pallas kernels: 36.2 us -> 35.1 us
    pallas_call x1, Pallas kernels: 36.2 us -> 35.1 us  [on_device(): pl.pallas_call(functools.partial(body, n_tile), out_shape=jax.ShapeDtypeS...]
where the time goes in v4:
time: 36.1 us; the launch traced here: 35.7 us
  Pallas kernels  35.1 us (97%)
  local copies, waits for them, and re-layouts  0.66 us (2%)
    pallas_call x1, Pallas kernels, on_device(): pl.pallas_call(functools.partial(body, n_tile), out_shape=jax.ShapeDtypeS...  35.1 us

profile of v4, /device:TPU:6, one launch (start us, length us, event | category | flops | bytes accessed | tf_op | source)
XLA Modules:
  0.0 35.7 jit_solution(454043510839497730)
XLA Ops:
  0.0 35.1 %shard_map.73 = f32[256,128]{1,0:T(8,128)S(1)} custom-call(f32[256,128]{1,0:T(8,128)} %bitcast.6, f32[24,8]{1,0:T(8,128)} %bitcast.7, f32[24,8]{1,0:T(8,128)} %bitcast.8, s32[24,128]{1,0:T(8,128)} %bitcast.9, s32[32]{0:T(128)} %fi.1, f32[32,32]{1,0:T(8,128)} %ke.1, s32[32,32]{1,0:T(8,128)} %ct.1), custom_call_target="tpu_custom_call" | custom-call | tf_op jit(solution)/shard_map/pallas_call | solution.py:390
  35.1 0.7 %copy.9 = f32[32,4,2,128]{3,2,1,0:T(2,128)} copy(f32[32,4,2,128]{3,2,1,0:T(2,128)S(1)} %bitcast.5) | data formatting | bytes 262144

commit v5 on v4

--- a/solution.py
+++ b/solution.py
@@ -296,12 +296,14 @@
 
     for i in range(2):
         moved_halo(1 - side_far, i).wait_recv()
-    leave(1 - side_far)
     turn(src2, side_far)
     for i, (x, reach) in enumerate(cells):
         moved = [[part[2 * i + l, pl.ds(8 * g, 8), :] for g in range(4)] for l in range(2)]
         pack(transport(src2, wbuf, x, steps[:reach], moved), x)
-    leave(side_far)
+    for half in range(2):
+        for k in range(SIDE):
+            for i in range(2):
+                spread(send2, recv2, s2_sem, r2_sem, 4 * plane(k) + zs[2 * half + i]).start()
 
     sources = [4 * plane(k) + lax.rem(z_me + quad // 2 + 3 + i, SIDE) for k in (3, 2, 1, 0) for i in range(SIDE)]
     for k in range(SIDE):

time: 36.1 us -> 36 us (level)
  no operation moved by 1% of the time
where the time goes in v5:
time: 36 us; the launch traced here: 35.6 us
  Pallas kernels  34.9 us (97%)
  local copies, waits for them, and re-layouts  0.66 us (2%)
    pallas_call x1, Pallas kernels, on_device(): pl.pallas_call(functools.partial(body, n_tile), out_shape=jax.ShapeDtypeS...  34.9 us

profile of v5, /device:TPU:6, one launch (start us, length us, event | category | flops | bytes accessed | tf_op | source)
XLA Modules:
  0.0 35.6 jit_solution(4702286180345495642)
XLA Ops:
  0.0 34.9 %shard_map.73 = f32[256,128]{1,0:T(8,128)S(1)} custom-call(f32[256,128]{1,0:T(8,128)} %bitcast.6, f32[24,8]{1,0:T(8,128)} %bitcast.7, f32[24,8]{1,0:T(8,128)} %bitcast.8, s32[24,128]{1,0:T(8,128)} %bitcast.9, s32[32]{0:T(128)} %fi.1, f32[32,32]{1,0:T(8,128)} %ke.1, s32[32,32]{1,0:T(8,128)} %ct.1), custom_call_target="tpu_custom_call" | custom-call | tf_op jit(solution)/shard_map/pallas_call | solution.py:392
  34.9 0.7 %copy.9 = f32[32,4,2,128]{3,2,1,0:T(2,128)} copy(f32[32,4,2,128]{3,2,1,0:T(2,128)S(1)} %bitcast.5) | data formatting | bytes 262144

commit v6 on v5

--- a/solution.py
+++ b/solution.py
@@ -205,8 +205,14 @@
         turn(src1, side)
 
     loads[3].wait()
-    for source in others:
-        arrived(frecv, fr_sem, fs_sem, source).wait_recv()
+    place = lax.rem(lane // 8 + 2 * sub, 16)
+    spots = [place, lax.rem(place + 15, 16), place]
+    frac = [zero, zero, zero]
+    for source in [me] + others[::-1]:
+        if source is not me:
+            arrived(frecv, fr_sem, fs_sem, source).wait_recv()
+        rows = [jnp.broadcast_to(frecv[source, i : i + 1, :], (8, 128)) for i in (0, 0, 1)]
+        frac = [jnp.where(spots[d] == source, rows[d], frac[d]) for d in range(3)]
 
     inner = (quad + 1) // 2 == 1
 
@@ -216,12 +222,6 @@
             known_sem, inc=1, device_id=(lax.rem(tile + n_tile - 1 + 2 * side_far, n_tile), me), device_id_type=MESH
         )
 
-    place = lax.rem(lane // 8 + 2 * sub, 16)
-    spots = [place, lax.rem(place + 15, 16), place]
-    frac = [zero, zero, zero]
-    for source in range(TRC):
-        rows = [jnp.broadcast_to(frecv[source, i : i + 1, :], (8, 128)) for i in (0, 0, 1)]
-        frac = [jnp.where(spots[d] == source, rows[d], frac[d]) for d in range(3)]
     frac[1] = pltpu.roll(frac[1], 120, 1)
     weights = []
     for d in range(3):

time: 36 us -> 36 us (level)
  no operation moved by 1% of the time
where the time goes in v6:
time: 36 us; the launch traced here: 35.4 us
  Pallas kernels  34.8 us (97%)
  local copies, waits for them, and re-layouts  0.66 us (2%)
    pallas_call x1, Pallas kernels, on_device(): pl.pallas_call(functools.partial(body, n_tile), out_shape=jax.ShapeDtypeS...  34.8 us

profile of v6, /device:TPU:6, one launch (start us, length us, event | category | flops | bytes accessed | tf_op | source)
XLA Modules:
  0.0 35.4 jit_solution(5862039426182937159)
XLA Ops:
  0.0 34.8 %shard_map.73 = f32[256,128]{1,0:T(8,128)S(1)} custom-call(f32[256,128]{1,0:T(8,128)} %bitcast.6, f32[24,8]{1,0:T(8,128)} %bitcast.7, f32[24,8]{1,0:T(8,128)} %bitcast.8, s32[24,128]{1,0:T(8,128)} %bitcast.9, s32[32]{0:T(128)} %fi.1, f32[32,32]{1,0:T(8,128)} %ke.1, s32[32,32]{1,0:T(8,128)} %ct.1), custom_call_target="tpu_custom_call" | custom-call | tf_op jit(solution)/shard_map/pallas_call | solution.py:392
  34.8 0.7 %copy.9 = f32[32,4,2,128]{3,2,1,0:T(2,128)} copy(f32[32,4,2,128]{3,2,1,0:T(2,128)S(1)} %bitcast.5) | data formatting | bytes 262144

commit v7 on v6

--- a/solution.py
+++ b/solution.py
@@ -192,9 +192,9 @@
     mirror = 127 - lane
     loads[6].wait()
 
-    def turn(buf, side):
+    def turn(buf, side, rows=range(4)):
         turned = jnp.full((8, 128), fl[lax.rem(tile + side, n_tile)], jnp.int32) == 1
-        for i in range(4):
+        for i in rows:
             for g in range(4):
                 at = (12 * side + i, pl.ds(8 * g, 8), slice(None))
                 v = buf[at]
@@ -296,7 +296,7 @@
 
     for i in range(2):
         moved_halo(1 - side_far, i).wait_recv()
-    turn(src2, side_far)
+        turn(src2, side_far, (2 * i, 2 * i + 1))
     for i, (x, reach) in enumerate(cells):
         moved = [[part[2 * i + l, pl.ds(8 * g, 8), :] for g in range(4)] for l in range(2)]
         pack(transport(src2, wbuf, x, steps[:reach], moved), x)

time: 36 us -> 36 us (level)
  no operation moved by 1% of the time
where the time goes in v7:
time: 36 us; the launch traced here: 35.4 us
  Pallas kernels  34.8 us (97%)
  local copies, waits for them, and re-layouts  0.66 us (2%)
    pallas_call x1, Pallas kernels, on_device(): pl.pallas_call(functools.partial(body, n_tile), out_shape=jax.ShapeDtypeS...  34.8 us

profile of v7, /device:TPU:6, one launch (start us, length us, event | category | flops | bytes accessed | tf_op | source)
XLA Modules:
  0.0 35.4 jit_solution(9802035925714971286)
XLA Ops:
  0.0 34.8 %shard_map.73 = f32[256,128]{1,0:T(8,128)S(1)} custom-call(f32[256,128]{1,0:T(8,128)} %bitcast.6, f32[24,8]{1,0:T(8,128)} %bitcast.7, f32[24,8]{1,0:T(8,128)} %bitcast.8, s32[24,128]{1,0:T(8,128)} %bitcast.9, s32[32]{0:T(128)} %fi.1, f32[32,32]{1,0:T(8,128)} %ke.1, s32[32,32]{1,0:T(8,128)} %ct.1), custom_call_target="tpu_custom_call" | custom-call | tf_op jit(solution)/shard_map/pallas_call | solution.py:392
  34.8 0.7 %copy.9 = f32[32,4,2,128]{3,2,1,0:T(2,128)} copy(f32[32,4,2,128]{3,2,1,0:T(2,128)S(1)} %bitcast.5) | data formatting | bytes 262144
